TPU v7x, 32 devices: a whole 2x2x4 slice. The times are simulated.
32 devices in a mesh: grp: 2 (over y), tile: 4 (over z), var: 4 (over x, core).
Axes of the slice: x: 2, y: 2, z: 4, core: 2. Of those that a mesh axis runs over, the one named last changes fastest.
Arguments:
- control: float32 [8, 128, 2048], P('var', ('grp', 'tile')), parts along dimension 1, may hold values from -6 to 6
- diffusivity: float32 [2, 128, 2048], P(None, ('grp', 'tile')), parts along dimension 1, may hold values from 0.05 to 0.95
- land_mask: int32 [128, 2048], P(('grp', 'tile')), parts along dimension 0, may hold values 0 or 1
- panel_tile: int32 [1024, 1], P(('grp', 'tile')), parts along dimension 0, may hold values from 0 to 3; in each aligned block of 128 rows (0 to 127, 128 to 255, ...) at most 64 rows name the same one
- panel_row: int32 [1024], P(('grp', 'tile')), parts along dimension 0, may hold values from 0 to 15
- panel_cols: int32 [1024, 128], P(('grp', 'tile')), parts along dimension 0, may hold values from 0 to 2047
- obs_values: float32 [1024, 128], P(('grp', 'tile')), parts along dimension 0, may hold values from -6 to 6
- obs_weights: float32 [1024, 128], P(('grp', 'tile')), parts along dimension 0, may hold values from 0.5 to 4
- panel_sensor: int32 [1024], P(('grp', 'tile')), parts along dimension 0, may hold values from 0 to 1
- sensitivity: float32 [2, 8], replicated, may hold values from 0.2 to 1
- cross_factor: float32 [8, 8], replicated, may hold values from -0.45 to 2
Outputs:
- gradient: float32 [8, 128, 2048], P('var', ('grp', 'tile')), parts along dimension 1
There are 2 independent parts, one for each index of `grp`. A program takes and returns all parts, laid end to end along the dimension named above; an argument that names none is the same for every part. Nothing has to cross between parts.
Inputs may be any that keep to these rules, and one draw needn't show every extreme that they name: `panel_tile`: among the 128 panels held by one tile index, at most 64 name the same tile.
All inputs are finite; a program needn't handle non-finite values. No bound on the sum of `land_mask` on one device may be relied on, other than what follows from the above.
Results may differ from a plain program's by a relative error of at most 0.00014.
Values sent between devices are 32-bit elements; how exact they have to be, the bound alone decides.
No kernel may reach another device: no remote copies, remote signals or barrier semaphores. Data moves between devices by JAX's collectives and lax.ppermute only.
A program may use at most 128 MiB of HBM per device.

v0:
```python
import functools

import jax
import jax.numpy as jnp
from jax import lax
from jax.experimental import pallas as pl
from jax.experimental.pallas import tpu as pltpu
from jax.sharding import PartitionSpec as P

PASSES = 10
LANES = 128
GROUP = 8
VMEM = pl.BlockSpec(memory_space=pltpu.VMEM)
SMEM = pl.BlockSpec(memory_space=pltpu.SMEM)
HBM = pl.BlockSpec(memory_space=pltpu.HBM)
AFTER = pl.BlockSpec(memory_space=pl.ANY)
F32 = jnp.float32


def in_hbm(values):
    return pltpu.with_memory_space_constraint(values, pltpu.HBM)


def call(body, outs, ins, scratch=(), limit=16, cost=None):
    return pl.pallas_call(
        body,
        out_shape=outs,
        in_specs=ins,
        out_specs=[VMEM] * len(outs),
        scratch_shapes=list(scratch),
        compiler_params=pltpu.CompilerParams(vmem_limit_bytes=limit << 20),
        cost_estimate=cost,
    )


def cost(cycles):
    return pl.CostEstimate(flops=cycles * 4096, bytes_accessed=cycles * 1024, transcendentals=0)


def response(sens_ref, factor_ref, sensor, variable):
    total = sens_ref[sensor, 0] * factor_ref[0, variable]
    for u in range(1, factor_ref.shape[0]):
        total = total + sens_ref[sensor, u] * factor_ref[u, variable]
    return total


def fetch(pairs, sems):
    copies = [pltpu.make_async_copy(src, dst, sems.at[i]) for i, (src, dst) in enumerate(pairs)]
    for copy in copies:
        copy.start()
    return copies


def first_kernel(slots, sens_hbm, factor_hbm, control_hbm, kappa_hbm, tile_hbm, row_hbm, sensor_hbm,
                 value_hbm, weight_hbm, cols_hbm, own_ref, other_ref, response_ref, kappa_ref, *refs):
    chunk_refs = refs[:-12]
    (sens_ref, factor_ref, control_ref, tile_ref, row_ref, sensor_ref, value_ref, weight_ref, cols_ref,
     send_ref, count_ref, sems) = refs[-12:]
    pairs = (
        (sens_hbm, sens_ref), (factor_hbm, factor_ref), (control_hbm, control_ref),
        (kappa_hbm, kappa_ref), (tile_hbm, tile_ref), (row_hbm, row_ref), (sensor_hbm, sensor_ref),
        (value_hbm, value_ref), (weight_hbm, weight_ref), (cols_hbm, cols_ref),
    )
    copies = [pltpu.make_async_copy(src, dst, sems.at[i]) for i, (src, dst) in enumerate(pairs)]
    for copy in copies:
        copy.start()
    send_ref[...] = jnp.zeros(send_ref.shape, F32)
    turns = len(chunk_refs)
    for turn in range(turns):
        count_ref[turn] = 0
    for copy in copies:
        copy.wait()

    member, mine = lax.axis_index("var"), lax.axis_index("tile")
    core = member % 2
    var_dev = control_ref.shape[0]
    for which, (sensor, out_ref) in enumerate(((core, own_ref), (1 - core, other_ref))):
        total = None
        for v in range(var_dev):
            scale = response(sens_ref, factor_ref, sensor, member * var_dev + v)
            response_ref[which, v] = jnp.full(response_ref.shape[2:], scale, F32)
            term = scale * control_ref[v]
            total = term if total is None else total + term
        out_ref[...] = total

    panels = value_ref.shape[0]
    sub = lax.broadcasted_iota(jnp.int32, (8 * turns, LANES), 0)
    lane = lax.broadcasted_iota(jnp.int32, (8 * turns, LANES), 1)
    trash = 3 * slots + 7

    def place(p, meta):
        turn = (tile_ref[p] ^ mine) - core * turns
        keep = (turn >= 0) & (turn < turns)
        turn = jnp.where(keep, turn, 0)
        slot = count_ref[turn]
        count_ref[turn] = slot + keep.astype(jnp.int32)
        rows = (value_ref[pl.ds(p, 1), :], weight_ref[pl.ds(p, 1), :], cols_ref[pl.ds(p, 1), :].astype(F32))
        for part, row in enumerate(rows):
            send_ref[turn, pl.ds(jnp.where(keep, part * slots + slot, trash), 1), :] = row
        facts = jnp.where(sub == 8 * turn, row_ref[p], sensor_ref[p]).astype(F32)
        here = (lane == jnp.where(keep, slot, LANES)) & (sub // 8 == turn)
        return jnp.where(here, facts, meta)

    meta = lax.fori_loop(0, panels, place, jnp.zeros((8 * turns, LANES), F32), unroll=8)
    for turn, chunk_ref in enumerate(chunk_refs):
        chunk_ref[: 3 * slots] = send_ref[turn, : 3 * slots]
        facts = meta[8 * turn : 8 * turn + 8]
        chunk_ref[3 * slots :] = jnp.where(lane[:8] == slots, count_ref[turn].astype(F32), facts)


def pieces(values):
    top = values.astype(jnp.bfloat16).astype(F32)
    return top, values - top


def scatter_kernel(slots, after_ref, home_ref, *refs):
    got_refs, (own_ref, other_ref, first_ref, acc_ref, meta_ref, sems) = refs[:-6], refs[-6:]
    core = lax.axis_index("var") % 2
    first_ref[...] = jnp.where(core == 0, home_ref[...], got_refs[0][...])
    got_refs = (first_ref, *got_refs[1:])
    copies = [
        pltpu.make_async_copy(ref.at[pl.ds(3 * slots, 8)], meta_ref.at[pl.ds(8 * s, 8)], sems.at[s])
        for s, ref in enumerate(got_refs)
    ]
    for copy in copies:
        copy.start()
    rows, width_cols = own_ref.shape[1:]
    blocks = width_cols // LANES
    acc_ref[...] = jnp.zeros(acc_ref.shape, F32)
    block_ids = lax.broadcasted_iota(jnp.int32, (blocks, LANES), 0)
    lane_ids = lax.broadcasted_iota(jnp.int32, (LANES, LANES), 0).astype(F32).astype(jnp.bfloat16)
    one, zero = jnp.bfloat16(1), jnp.bfloat16(0)
    sub = lax.broadcasted_iota(jnp.int32, (GROUP, LANES), 0)
    for copy in copies:
        copy.wait()

    def source(s, got_ref):
        count = meta_ref[8 * s, slots].astype(jnp.int32)

        def group(g, carry):
            base = pl.multiple_of(g * GROUP, GROUP)
            value = got_ref[pl.ds(base, GROUP), :]
            weight = got_ref[pl.ds(slots + base, GROUP), :]
            cell = got_ref[pl.ds(2 * slots + base, GROUP), :].astype(jnp.int32)
            weight = jnp.where(sub + base < count, weight, 0.0)
            parts = pieces(weight) + pieces(weight * value)
            low = (cell % LANES).astype(F32)
            high = cell // LANES
            for k in range(GROUP):
                in_block = block_ids == high[k : k + 1]
                left = jnp.concatenate(
                    [jnp.where(in_block, parts[i][k : k + 1], 0.0) for i in (0, 2, 1, 3)], axis=0
                ).astype(jnp.bfloat16)
                column = jnp.broadcast_to(low[k : k + 1], (16, LANES)).astype(jnp.bfloat16)
                right = jnp.where(lane_ids == jnp.concatenate([column] * (LANES // 16), axis=0), one, zero)
                both = lax.dot_general(
                    left, right, (((1,), (1,)), ((), ())), preferred_element_type=F32
                )
                row = meta_ref[8 * s, base + k].astype(jnp.int32)
                sensor = meta_ref[8 * s + 1, base + k].astype(jnp.int32)
                at = pl.multiple_of((sensor * rows + row) * 2 * blocks, 2 * blocks)
                acc_ref[pl.ds(at, 2 * blocks), :] += both[: 2 * blocks] + both[2 * blocks :]
            return carry

        lax.fori_loop(0, (count + GROUP - 1) // GROUP, group, 0)

    for s, got_ref in enumerate(got_refs):
        source(s, got_ref)
    for sensor, out_ref in ((core, own_ref), (1 - core, other_ref)):
        start = sensor * rows * 2 * blocks
        for kind in range(2):
            for b in range(blocks):
                out_ref[kind, :, b * LANES : (b + 1) * LANES] = acc_ref[
                    pl.ds(start + kind * blocks + b, rows, stride=2 * blocks), :
                ]


def even_tile():
    return lax.axis_index("tile") % 2 == 0


def has_above():
    return lax.axis_index("tile") > 0


def has_below():
    return lax.axis_index("tile") + 1 < lax.axis_size("tile")


def pack_edges(even_ref, odd_ref, rows_value, margin):
    rows, width = rows_value.shape
    even = even_tile()
    for b in range(width // LANES):
        at = slice(b * LANES, (b + 1) * LANES)
        head, tail = rows_value[:margin, at], rows_value[rows - margin :, at]
        even_ref[b * margin : (b + 1) * margin] = jnp.where(even, tail, head)
        odd_ref[b * margin : (b + 1) * margin] = jnp.where(even, head, tail)


def edges_kernel(margin, first_ref, second_ref, kappa_ref, *refs):
    total_ref, even_ref, odd_ref = refs[-3:]
    total = first_ref[...] + second_ref[...]
    total_ref[...] = total
    for i, field in enumerate((total, kappa_ref[0], kappa_ref[1])):
        pack_edges(even_ref.at[i], odd_ref.at[i], field, margin)


def ring_rows(rows, margin):
    return -(-(rows + 2 * margin) // 8) * 8


def lay_ring(ref, own, from_even, from_odd, margin):
    rows, total = own.shape[0], ref.shape[0]
    even = even_tile()
    ref[rows:total] = jnp.zeros((total - rows, ref.shape[1]), F32)
    ref[:rows] = own
    for b in range(ref.shape[1] // LANES):
        at = slice(b * LANES, (b + 1) * LANES)
        one, two = (m[b * margin : (b + 1) * margin] for m in (from_even, from_odd))
        ref[rows : rows + margin, at] = jnp.where(has_below(), jnp.where(even, one, two), 0.0)
        ref[total - margin :, at] = jnp.where(has_above(), jnp.where(even, two, one), 0.0)


def block(ref, j):
    return ref[:, j * LANES : (j + 1) * LANES]


def sideways(blocks):
    shape = blocks[0].shape
    lane = lax.broadcasted_iota(jnp.int32, shape, 1)
    zero = jnp.zeros(shape, F32)
    ahead = [pltpu.roll(x, 1, 1) for x in blocks]
    back = [pltpu.roll(x, LANES - 1, 1) for x in blocks]
    for j, here in enumerate(blocks):
        before = ahead[j - 1] if j else zero
        after = back[j + 1] if j + 1 < len(blocks) else zero
        yield here, jnp.where(lane == 0, before, ahead[j]), jnp.where(lane == LANES - 1, after, back[j])


def face_weights(coef_ref, row_ref, col_ref, rows, margin):
    total, width = row_ref.shape
    blocks = width // LANES
    r = lax.broadcasted_iota(jnp.int32, (total, LANES), 0)
    inside = (
        (r < rows)
        | ((r < rows + margin) & has_below())
        | ((r >= total - margin) & has_above())
    )
    scale = jnp.where(inside, 0.125, 0.0)
    unit = jnp.where(inside, 1.0, 0.0)
    columns = [block(col_ref, j) for j in range(blocks)]
    for j, (k_col, k_left, k_right) in enumerate(sideways(columns)):
        at = slice(j * LANES, (j + 1) * LANES)
        k_row = block(row_ref, j)
        up = scale * (k_row + pltpu.roll(k_row, 1, 0))
        down = scale * (k_row + pltpu.roll(k_row, total - 1, 0))
        left = scale * (k_col + k_left)
        right = scale * (k_col + k_right)
        coef_ref[0, :, at] = unit - up - down - left - right
        coef_ref[1, :, at] = up
        coef_ref[2, :, at] = down
        coef_ref[3, :, at] = left
        coef_ref[4, :, at] = right


def one_pass(source_ref, target_ref, coef_ref, spans, keep):
    width = source_ref.shape[1]

    def read(ref, *lead, at):
        got = [ref[(*lead, span, at)] for span in spans]
        return jnp.concatenate(got, axis=0) if len(got) > 1 else got[0]

    sections = [slice(j * LANES, (j + 1) * LANES) for j in range(width // LANES)]
    fields = [read(source_ref, at=at) for at in sections]
    total = fields[0].shape[0]
    for at, (here, left, right) in zip(sections, sideways(fields)):
        new = (
            read(coef_ref, 0, at=at) * here
            + read(coef_ref, 1, at=at) * pltpu.roll(here, 1, 0)
            + read(coef_ref, 2, at=at) * pltpu.roll(here, total - 1, 0)
            + read(coef_ref, 3, at=at) * left
            + read(coef_ref, 4, at=at) * right
        )
        start = 0
        for span in spans[:keep]:
            size = span.stop - span.start
            target_ref[span, at] = new[start : start + size]
            start += size


def diffuse(one_ref, two_ref, coef_ref, rows, margin):
    total = one_ref.shape[0]
    wide = [slice(0, total)]
    inner = margin // 8 * 8
    narrow = [slice(0, rows), slice(rows, rows + inner), slice(total - inner, total)]
    first = (margin - inner + 1) // 2

    def twice(spans, index, carry):
        one_pass(one_ref, two_ref, coef_ref, spans, len(spans))
        one_pass(two_ref, one_ref, coef_ref, spans, len(spans))
        return carry

    for i in range(first):
        twice(wide, i, 0)
    lax.fori_loop(0, PASSES // 2 - first - 1, functools.partial(twice, narrow), 0)
    one_pass(one_ref, two_ref, coef_ref, narrow, 3)
    one_pass(two_ref, one_ref, coef_ref, narrow, 1)


def faces_kernel(margin, even_ref, odd_ref, kappa_ref, sums_ref, coef_ref, sums_out, one_ref, two_ref):
    sums_out[...] = sums_ref[...]
    rows = kappa_ref.shape[1]
    lay_ring(one_ref, kappa_ref[0], even_ref.at[1], odd_ref.at[1], margin)
    lay_ring(two_ref, kappa_ref[1], even_ref.at[2], odd_ref.at[2], margin)
    face_weights(coef_ref, one_ref, two_ref, rows, margin)


def smooth_kernel(margin, own_ref, even_ref, odd_ref, coef_ref, out_ref, one_ref, two_ref):
    rows = own_ref.shape[0]
    lay_ring(one_ref, own_ref[...], even_ref.at[0], odd_ref.at[0], margin)
    diffuse(one_ref, two_ref, coef_ref, rows, margin)
    out_ref[...] = one_ref[:rows]


def adjoint_kernel(margin, smooth_ref, mask_ref, sums_ref, more_ref, adjoint_ref, even_ref, odd_ref):
    weight = sums_ref[0] + more_ref[0]
    value = sums_ref[1] + more_ref[1]
    adjoint = mask_ref[...].astype(F32) * (weight * smooth_ref[...] - value)
    adjoint_ref[...] = adjoint
    pack_edges(even_ref, odd_ref, adjoint, margin)


def spread_kernel(margin, own_ref, even_ref, odd_ref, coef_ref, out_ref, one_ref, two_ref):
    rows = own_ref.shape[0]
    lay_ring(one_ref, own_ref[...], even_ref, odd_ref, margin)
    diffuse(one_ref, two_ref, coef_ref, rows, margin)
    out_ref[...] = one_ref[:rows]


def result_kernel(response_ref, control_ref, own_ref, other_ref, out_ref):
    for v in range(control_ref.shape[0]):
        mine, theirs = (response_ref[i, v][:1, :1] for i in range(2))
        out_ref[v] = control_ref[v] + mine * own_ref[...] + theirs * other_ref[...]


def swap(values, axis, bit):
    count = lax.axis_size(axis)
    return lax.ppermute(values, axis, [(i, i ^ bit) for i in range(count)])


def swap_edges(even, odd):
    tiles, members = lax.axis_size("tile"), lax.axis_size("var")
    pairs = []
    for t in range(tiles):
        other = t + 1 if t % 2 else t - 1
        for q in range(members):
            to = other * members + q if 0 <= other < tiles else t * members + (q ^ 1)
            pairs.append((t * members + q, to))
    return swap(even, "tile", 1), lax.ppermute(odd, ("tile", "var"), pairs)


def combine(values, members, first):
    bit = first
    while 2 * bit < members:
        values = values + swap(values, "var", bit)
        bit *= 2
    return values, swap(values, "var", bit)


def deliver(chunk, turn):
    tiles, members = lax.axis_size("tile"), lax.axis_size("var")
    pairs = []
    for t in range(tiles):
        for q in range(members):
            offset = (q % 2) * (tiles // 2) + turn
            pairs.append((t * members + q, (t ^ max(offset, 1)) * members + q))
    return lax.ppermute(chunk, ("tile", "var"), pairs)


def local(control, diffusivity, land_mask, panel_tile, panel_row, panel_cols, obs_values,
          obs_weights, panel_sensor, sensitivity, cross_factor):
    rows, width = control.shape[1:]
    var_dev = control.shape[0]
    tiles, members = lax.axis_size("tile"), lax.axis_size("var")
    panels, panel_width = panel_cols.shape
    slots = 2 * panels // tiles
    turns = tiles // 2
    blocks = width // LANES
    margin = PASSES
    total = ring_rows(rows, margin)
    field = jax.ShapeDtypeStruct((rows, width), F32)
    field2 = jax.ShapeDtypeStruct((2, rows, width), F32)
    edge = jax.ShapeDtypeStruct((margin * blocks, LANES), F32)
    edge3 = jax.ShapeDtypeStruct((3, margin * blocks, LANES), F32)
    chunk = jax.ShapeDtypeStruct((3 * slots + 8, panel_width), F32)
    ints = pltpu.SMEM((panels,), jnp.int32)

    own, other, responses, kappa, *chunks = call(
        functools.partial(first_kernel, slots),
        [field, field, jax.ShapeDtypeStruct((2, var_dev, 8, LANES), F32), field2] + [chunk] * turns,
        [HBM] * 10,
        [
            pltpu.SMEM(sensitivity.shape, F32),
            pltpu.SMEM(cross_factor.shape, F32),
            pltpu.VMEM(control.shape, F32),
            ints, ints, ints,
            pltpu.VMEM(obs_values.shape, F32),
            pltpu.VMEM(obs_weights.shape, F32),
            pltpu.VMEM(panel_cols.shape, jnp.int32),
            pltpu.VMEM((turns, *chunk.shape), F32),
            pltpu.SMEM((turns,), jnp.int32),
            pltpu.SemaphoreType.DMA((10,)),
        ],
        cost=cost(3000),
    )(*(in_hbm(x) for x in (sensitivity, cross_factor, control, diffusivity, panel_tile.reshape(-1),
                            panel_row, panel_sensor, obs_values, obs_weights, panel_cols)))

    got = [deliver(c, turn) for turn, c in enumerate(chunks)]
    part, more = combine(own + swap(other, "var", 1), members, 2)
    smooth_in, even, odd = call(
        functools.partial(edges_kernel, margin),
        [field, edge3, edge3],
        [VMEM] * 3 + [AFTER] * turns,
        cost=cost(500),
    )(part, more, kappa, *got)
    even, odd = swap_edges(even, odd)
    sums, sums_other = call(
        functools.partial(scatter_kernel, slots),
        [field2, field2],
        [AFTER] + [VMEM] * (turns + 1),
        [
            pltpu.VMEM(chunk.shape, F32),
            pltpu.VMEM((2 * rows * 2 * blocks, LANES), F32),
            pltpu.SMEM((8 * turns, LANES), F32),
            pltpu.SemaphoreType.DMA((turns,)),
        ],
        cost=cost(10000),
    )(smooth_in, chunks[0], *got)
    ring = pltpu.VMEM((total, width), F32)
    coef, sums_other = call(
        functools.partial(faces_kernel, margin),
        [jax.ShapeDtypeStruct((5, total, width), F32), field2],
        [VMEM] * 4,
        [ring, ring],
        cost=cost(1000),
    )(even, odd, kappa, sums_other)
    more_sums = swap(sums_other, "var", 1)
    (smooth,) = call(
        functools.partial(smooth_kernel, margin),
        [field],
        [VMEM] * 4,
        [ring, ring],
        cost=cost(4000),
    )(smooth_in, even, odd, coef)
    adjoint, even, odd = call(
        functools.partial(adjoint_kernel, margin), [field, edge, edge], [VMEM] * 4, cost=cost(500)
    )(smooth, land_mask, sums, more_sums)
    even, odd = swap_edges(even, odd)
    (mine,) = call(
        functools.partial(spread_kernel, margin),
        [field],
        [VMEM] * 4,
        [ring, ring],
        cost=cost(4000),
    )(adjoint, even, odd, coef)
    (out,) = call(
        result_kernel,
        [jax.ShapeDtypeStruct(control.shape, F32)],
        [VMEM] * 4,
        cost=cost(1000),
    )(responses, control, mine, swap(mine, "var", 1))
    return out


def solution(mesh):
    return jax.shard_map(
        local,
        mesh=mesh,
        in_specs=(
            P("var", ("grp", "tile"), None),
            P(None, ("grp", "tile"), None),
            P(("grp", "tile"), None),
            P(("grp", "tile"), None),
            P(("grp", "tile")),
            P(("grp", "tile"), None),
            P(("grp", "tile"), None),
            P(("grp", "tile"), None),
            P(("grp", "tile")),
            P(),
            P(),
        ),
        out_specs=P("var", ("grp", "tile"), None),
        check_vma=False,
    )
```

profile of v0, /device:TPU:0, one launch (start us, length us, event | category | flops | bytes accessed | tf_op | source)
XLA Modules:
  0.0 35.2 jit_solution(2783882727529138754)
XLA Ops:
  0.0 2.5 %shard_map.109 = (f32[16,2048]{1,0:T(8,128)S(1)}, f32[16,2048]{1,0:T(8,128)S(1)}, f32[2,2,8,128]{3,2,1,0:T(8,128)S(1)}, f32[2,16,2048]{2,1,0:T(8,128)S(1)}, f32[...) custom-call(f32[2,8]{1,0:T(2,128)} %sens_hbm.1, f32[8,8]{1,0:T(8,128)} %factor_hbm.1, f32[2,16,2048]{2,1,0:T(8,128)} %control_ref.1, ...), custom_call_target="tpu_custom_call" | custom-call | flops 12288000 | bytes 3072000 | tf_op jit(solution)/shard_map/pallas_call | solution.py:398
  2.5 0.5 %collective-permute-start = (f32[16,2048]{1,0:T(8,128)S(1)}, f32[16,2048]{1,0:T(8,128)S(1)}, u32[]{:S(2)}, u32[]{:S(2)}) collective-permute-start(f32[16,2048]{1,0:T(8,128)S(1)} %get-tuple-element.23), channel_id=1, source_target_pairs={{0,1},{1,0},{2,3},{3,2},{4,5},{5,4},{6,7},{7,6},{8,9},{9,8},{10,11... | collective-permute-start | bytes 393224 | tf_op jit(solution)/shard_map/ppermute | solution.py:348
  3.0 1.0 %collective-permute-done = f32[16,2048]{1,0:T(8,128)S(1)} collective-permute-done((f32[16,2048]{1,0:T(8,128)S(1)}, f32[16,2048]{1,0:T(8,128)S(1)}, u32[]{:S(2)}, u32[]{:S(2)}) %collective-permute-start) | collective-permute-done | bytes 131104 | tf_op jit(solution)/shard_map/ppermute | solution.py:348
  4.0 2.9 %collective-permute-start.1 = (f32[16,2048]{1,0:T(8,128)S(1)}, f32[16,2048]{1,0:T(8,128)S(1)}, u32[]{:S(2)}, u32[]{:S(2)}) collective-permute-start(f32[16,2048]{1,0:T(8,128)S(1)} %add.3.first_ref), channel_id=1, source_target_pairs={{0,2},{1,3},{2,0},{3,1},{4,6},{5,7},{6,4},{7,5},{8,10},{9,11},{10,... | collective-permute-start | bytes 393224 | tf_op jit(solution)/shard_map/ppermute | solution.py:348
  6.9 1.6 %collective-permute-start.3 = (f32[200,128]{1,0:T(8,128)S(1)}, f32[200,128]{1,0:T(8,128)S(1)}, u32[]{:S(2)}, u32[]{:S(2)}) collective-permute-start(f32[200,128]{1,0:T(8,128)S(1)} %get-tuple-element.26), channel_id=1, source_target_pairs={{0,4},{1,13},{2,6},{3,15},{4,0},{5,9},{6,2},{7,11},{8,12},{9,5},{1... | collective-permute-start | bytes 307208 | tf_op jit(solution)/shard_map/ppermute | solution.py:377
  8.5 0.4 %collective-permute-start.2 = (f32[200,128]{1,0:T(8,128)S(1)}, f32[200,128]{1,0:T(8,128)S(1)}, u32[]{:S(2)}, u32[]{:S(2)}) collective-permute-start(f32[200,128]{1,0:T(8,128)S(1)} %get-tuple-element.25.home_ref), channel_id=1, source_target_pairs={{0,4},{1,9},{2,6},{3,11},{4,0},{5,13},{6,2},{7,15},{8,12},{9,1},{1... | collective-permute-start | bytes 307208 | tf_op jit(solution)/shard_map/ppermute | solution.py:377
  8.9 3.7 %collective-permute-done.3.refs_1_ = f32[200,128]{1,0:T(8,128)S(1)} collective-permute-done((f32[200,128]{1,0:T(8,128)S(1)}, f32[200,128]{1,0:T(8,128)S(1)}, u32[]{:S(2)}, u32[]{:S(2)}) %collective-permute-start.3) | collective-permute-done | bytes 102432 | tf_op jit(solution)/shard_map/ppermute | solution.py:377
  12.7 1.3 %collective-permute-done.2.refs_0_ = f32[200,128]{1,0:T(8,128)S(1)} collective-permute-done((f32[200,128]{1,0:T(8,128)S(1)}, f32[200,128]{1,0:T(8,128)S(1)}, u32[]{:S(2)}, u32[]{:S(2)}) %collective-permute-start.2) | collective-permute-done | bytes 102432 | tf_op jit(solution)/shard_map/ppermute | solution.py:377
  13.9 0.0 collective-permute-done.1.second_ref
  13.9 0.1 shard_map.110
  14.0 1.7 %collective-permute-start.4 = (f32[3,160,128]{2,1,0:T(8,128)S(1)}, f32[3,160,128]{2,1,0:T(8,128)S(1)}, u32[]{:S(2)}, u32[]{:S(2)}) collective-permute-start(f32[3,160,128]{2,1,0:T(8,128)S(1)} %get-tuple-element.28), channel_id=1, source_target_pairs={{0,4},{4,0},{8,12},{12,8},{1,5},{5,1},{9,13},{13,9},{2,6},{6,2},{1... | collective-permute-start | bytes 737288 | tf_op jit(solution)/shard_map/ppermute | solution.py:348
  15.7 0.0 collective-permute-start.5
  15.7 2.8 %shard_map.111 = (f32[2,16,2048]{2,1,0:T(8,128)S(1)}, f32[2,16,2048]{2,1,0:T(8,128)S(1)}) custom-call(f32[16,2048]{1,0:T(8,128)S(1)} %get-tuple-element.27.after_ref.own_ref, f32[200,128]{1,0:T(8,128)S(1)} %get-tuple-element.25.home_ref, f32[200,128]{1,0:T(8,128)S(1)} %collective-permute-done.2.refs_0_, f32[200,128]{1,0:T(8,128)S(1)} %collective-permute-done.3.refs_1_), custom_call_target="tpu_custom_call" | custom-call | flops 40960000 | bytes 10240000 | tf_op jit(solution)/shard_map/pallas_call | solution.py:427
  18.5 4.2 %collective-permute-done.4.even_ref = f32[3,160,128]{2,1,0:T(8,128)S(1)} collective-permute-done((f32[3,160,128]{2,1,0:T(8,128)S(1)}, f32[3,160,128]{2,1,0:T(8,128)S(1)}, u32[]{:S(2)}, u32[]{:S(2)}) %collective-permute-start.4) | collective-permute-done | bytes 245792 | tf_op jit(solution)/shard_map/ppermute | solution.py:348
  22.7 0.0 collective-permute-done.5.odd_ref
  22.7 0.0 copy-start.1
  22.7 0.3 shard_map.112
  23.1 0.2 collective-permute-start.6
  23.2 1.9 %shard_map.113.smooth_ref = f32[16,2048]{1,0:T(8,128)S(1)} custom-call(f32[16,2048]{1,0:T(8,128)S(1)} %get-tuple-element.27.after_ref.own_ref, f32[3,160,128]{2,1,0:T(8,128)S(1)} %collective-permute-done.4.even_ref, f32[3,160,128]{2,1,0:T(8,128)S(1)} %collective-permute-done.5.odd_ref, f32[5,40,2048]{2,1,0:T(8,128)S(1)} %get-tuple-element.31.coef_ref), custom_call_target="tpu_custom_call" | custom-call | flops 16384000 | bytes 4096000 | tf_op jit(solution)/shard_map/pallas_call | solution.py:448
  25.2 0.0 copy-start
  25.2 0.0 collective-permute-done.6.more_ref
  25.2 0.0 copy-done.1
  25.2 0.1 shard_map.114
  25.3 2.7 %collective-permute-start.7 = (f32[160,128]{1,0:T(8,128)S(1)}, f32[160,128]{1,0:T(8,128)S(1)}, u32[]{:S(2)}, u32[]{:S(2)}) collective-permute-start(f32[160,128]{1,0:T(8,128)S(1)} %get-tuple-element.35), channel_id=1, source_target_pairs={{0,4},{4,0},{8,12},{12,8},{1,5},{5,1},{9,13},{13,9},{2,6},{6,2},{1... | collective-permute-start | bytes 245768 | tf_op jit(solution)/shard_map/ppermute | solution.py:348
  28.0 0.2 collective-permute-start.8
  28.2 2.9 %collective-permute-done.7.even_ref = f32[160,128]{1,0:T(8,128)S(1)} collective-permute-done((f32[160,128]{1,0:T(8,128)S(1)}, f32[160,128]{1,0:T(8,128)S(1)}, u32[]{:S(2)}, u32[]{:S(2)}) %collective-permute-start.7) | collective-permute-done | bytes 81952 | tf_op jit(solution)/shard_map/ppermute | solution.py:348
  31.1 0.0 collective-permute-done.8.odd_ref
  31.1 1.9 %shard_map.115.own_ref = f32[16,2048]{1,0:T(8,128)S(1)} custom-call(f32[16,2048]{1,0:T(8,128)S(1)} %get-tuple-element.34.own_ref, f32[160,128]{1,0:T(8,128)S(1)} %collective-permute-done.7.even_ref, f32[160,128]{1,0:T(8,128)S(1)} %collective-permute-done.8.odd_ref, f32[5,40,2048]{2,1,0:T(8,128)S(1)} %get-tuple-element.31.coef_ref), custom_call_target="tpu_custom_call" | custom-call | flops 16384000 | bytes 4096000 | tf_op jit(solution)/shard_map/pallas_call | solution.py:459
  33.0 0.1 collective-permute-start.9
  33.1 1.3 %collective-permute-done.9.other_ref = f32[16,2048]{1,0:T(8,128)S(1)} collective-permute-done((f32[16,2048]{1,0:T(8,128)S(1)}, f32[16,2048]{1,0:T(8,128)S(1)}, u32[]{:S(2)}, u32[]{:S(2)}) %collective-permute-start.9) | collective-permute-done | bytes 131104 | tf_op jit(solution)/shard_map/ppermute | solution.py:348
  34.4 0.0 copy-done
  34.4 0.8 %shard_map.116 = f32[2,16,2048]{2,1,0:T(8,128)} custom-call(f32[2,2,8,128]{3,2,1,0:T(8,128)S(1)} %get-tuple-element.21.response_ref, f32[2,16,2048]{2,1,0:T(8,128)S(1)} %copy-done, f32[16,2048]{1,0:T(8,128)S(1)} %shard_map.115.own_ref, f32[16,2048]{1,0:T(8,128)S(1)} %collective-permute-done.9.other_ref), custom_call_target="tpu_custom_call" | custom-call | flops 4096000 | bytes 1024000 | tf_op jit(solution)/shard_map/pallas_call | solution.py:466
  (1 shorter events, 0.0 us)
Async XLA Ops:
  2.5 1.5 %collective-permute-start = (f32[16,2048]{1,0:T(8,128)S(1)}, f32[16,2048]{1,0:T(8,128)S(1)}, u32[]{:S(2)}, u32[]{:S(2)}) collective-permute-start(f32[16,2048]{1,0:T(8,128)S(1)} %get-tuple-element.23), channel_id=1, source_target_pairs={{0,1},{1,0},{2,3},{3,2},{4,5},{5,4},{6,7},{7,6},{8,9},{9,8},{10,11... | collective-permute-start | bytes 393224 | tf_op jit(solution)/shard_map/ppermute | solution.py:348
  4.0 9.9 %collective-permute-start.1 = (f32[16,2048]{1,0:T(8,128)S(1)}, f32[16,2048]{1,0:T(8,128)S(1)}, u32[]{:S(2)}, u32[]{:S(2)}) collective-permute-start(f32[16,2048]{1,0:T(8,128)S(1)} %add.3.first_ref), channel_id=1, source_target_pairs={{0,2},{1,3},{2,0},{3,1},{4,6},{5,7},{6,4},{7,5},{8,10},{9,11},{10,... | collective-permute-start | bytes 393224 | tf_op jit(solution)/shard_map/ppermute | solution.py:348
  6.9 5.8 %collective-permute-start.3 = (f32[200,128]{1,0:T(8,128)S(1)}, f32[200,128]{1,0:T(8,128)S(1)}, u32[]{:S(2)}, u32[]{:S(2)}) collective-permute-start(f32[200,128]{1,0:T(8,128)S(1)} %get-tuple-element.26), channel_id=1, source_target_pairs={{0,4},{1,13},{2,6},{3,15},{4,0},{5,9},{6,2},{7,11},{8,12},{9,5},{1... | collective-permute-start | bytes 307208 | tf_op jit(solution)/shard_map/ppermute | solution.py:377
  8.5 5.4 %collective-permute-start.2 = (f32[200,128]{1,0:T(8,128)S(1)}, f32[200,128]{1,0:T(8,128)S(1)}, u32[]{:S(2)}, u32[]{:S(2)}) collective-permute-start(f32[200,128]{1,0:T(8,128)S(1)} %get-tuple-element.25.home_ref), channel_id=1, source_target_pairs={{0,4},{1,9},{2,6},{3,11},{4,0},{5,13},{6,2},{7,15},{8,12},{9,1},{1... | collective-permute-start | bytes 307208 | tf_op jit(solution)/shard_map/ppermute | solution.py:377
  14.0 8.7 %collective-permute-start.4 = (f32[3,160,128]{2,1,0:T(8,128)S(1)}, f32[3,160,128]{2,1,0:T(8,128)S(1)}, u32[]{:S(2)}, u32[]{:S(2)}) collective-permute-start(f32[3,160,128]{2,1,0:T(8,128)S(1)} %get-tuple-element.28), channel_id=1, source_target_pairs={{0,4},{4,0},{8,12},{12,8},{1,5},{5,1},{9,13},{13,9},{2,6},{6,2},{1... | collective-permute-start | bytes 737288 | tf_op jit(solution)/shard_map/ppermute | solution.py:348
  15.7 7.0 %collective-permute-start.5 = (f32[3,160,128]{2,1,0:T(8,128)S(1)}, f32[3,160,128]{2,1,0:T(8,128)S(1)}, u32[]{:S(2)}, u32[]{:S(2)}) collective-permute-start(f32[3,160,128]{2,1,0:T(8,128)S(1)} %get-tuple-element.29), channel_id=1, source_target_pairs={{0,1},{1,0},{2,3},{3,2},{4,8},{5,9},{6,10},{7,11},{8,4},{9,5},{10,... | collective-permute-start | bytes 737288 | tf_op jit(solution)/shard_map/ppermute | solution.py:359
  22.7 2.5 %copy-start.1 = (s32[16,2048]{1,0:T(8,128)S(1)}, s32[16,2048]{1,0:T(8,128)}, u32[]{:S(2)}) copy-start(s32[16,2048]{1,0:T(8,128)} %mask_ref.1) | copy-start | bytes 393220
  23.1 2.1 %collective-permute-start.6 = (f32[2,16,2048]{2,1,0:T(8,128)S(1)}, f32[2,16,2048]{2,1,0:T(8,128)S(1)}, u32[]{:S(2)}, u32[]{:S(2)}) collective-permute-start(f32[2,16,2048]{2,1,0:T(8,128)S(1)} %get-tuple-element.33), channel_id=1, source_target_pairs={{0,1},{1,0},{2,3},{3,2},{4,5},{5,4},{6,7},{7,6},{8,9},{9,8},{10,11... | collective-permute-start | bytes 786440 | tf_op jit(solution)/shard_map/ppermute | solution.py:348
  25.2 9.3 %copy-start = (f32[2,16,2048]{2,1,0:T(8,128)S(1)}, f32[2,16,2048]{2,1,0:T(8,128)}, u32[]{:S(2)}) copy-start(f32[2,16,2048]{2,1,0:T(8,128)} %control_ref.1) | copy-start | bytes 786436
  25.3 5.8 %collective-permute-start.7 = (f32[160,128]{1,0:T(8,128)S(1)}, f32[160,128]{1,0:T(8,128)S(1)}, u32[]{:S(2)}, u32[]{:S(2)}) collective-permute-start(f32[160,128]{1,0:T(8,128)S(1)} %get-tuple-element.35), channel_id=1, source_target_pairs={{0,4},{4,0},{8,12},{12,8},{1,5},{5,1},{9,13},{13,9},{2,6},{6,2},{1... | collective-permute-start | bytes 245768 | tf_op jit(solution)/shard_map/ppermute | solution.py:348
  28.0 3.1 %collective-permute-start.8 = (f32[160,128]{1,0:T(8,128)S(1)}, f32[160,128]{1,0:T(8,128)S(1)}, u32[]{:S(2)}, u32[]{:S(2)}) collective-permute-start(f32[160,128]{1,0:T(8,128)S(1)} %get-tuple-element.36), channel_id=1, source_target_pairs={{0,1},{1,0},{2,3},{3,2},{4,8},{5,9},{6,10},{7,11},{8,4},{9,5},{10,... | collective-permute-start | bytes 245768 | tf_op jit(solution)/shard_map/ppermute | solution.py:359
  33.0 1.4 %collective-permute-start.9 = (f32[16,2048]{1,0:T(8,128)S(1)}, f32[16,2048]{1,0:T(8,128)S(1)}, u32[]{:S(2)}, u32[]{:S(2)}) collective-permute-start(f32[16,2048]{1,0:T(8,128)S(1)} %shard_map.115.own_ref), channel_id=1, source_target_pairs={{0,1},{1,0},{2,3},{3,2},{4,5},{5,4},{6,7},{7,6},{8,9},{9,8},{10,11... | collective-permute-start | bytes 393224 | tf_op jit(solution)/shard_map/ppermute | solution.py:348
where the time goes:
time: 35.4 us; the launch traced here: 35.2 us
  waiting for transfers between devices  14.4 us (41%)
  Pallas kernels  10.4 us (29%)
  starting transfers between devices  10.3 us (29%)
    ppermute x6, waiting for transfers between devices, swap(): return lax.ppermute(values, axis, [(i, i ^ bit) for i in range(count)])  9.42 us
    ppermute x6, starting transfers between devices, swap(): return lax.ppermute(values, axis, [(i, i ^ bit) for i in range(count)])  8.03 us
    ppermute x2, waiting for transfers between devices, deliver(): return lax.ppermute(chunk, ('tile', 'var'), pairs)  4.99 us
    pallas_call x1, Pallas kernels, local(): call(functools.partial(scatter_kernel, slots), [field2, field2], [AFTER]...  2.82 us
    pallas_call x1, Pallas kernels, local(): call(functools.partial(first_kernel, slots), [field, field, jax.ShapeDtyp...  2.46 us
    ppermute x2, starting transfers between devices, deliver(): return lax.ppermute(chunk, ('tile', 'var'), pairs)  2.03 us
    pallas_call x1, Pallas kernels, local(): call(functools.partial(smooth_kernel, margin), [field], [VMEM] * 4, [ring...  1.94 us
    pallas_call x1, Pallas kernels, local(): call(functools.partial(spread_kernel, margin), [field], [VMEM] * 4, [ring...  1.93 us
  transfers between devices with their start and end apart: 10, of which 6 were waited for; matrix products, arithmetic and copies ran while one was open for 0% of the time, Pallas kernels for 14%

commit v1 on v0

--- a/solution.py
+++ b/solution.py
@@ -9,7 +9,7 @@
 
 PASSES = 10
 LANES = 128
-GROUP = 8
+GROUP = 16
 VMEM = pl.BlockSpec(memory_space=pltpu.VMEM)
 SMEM = pl.BlockSpec(memory_space=pltpu.SMEM)
 HBM = pl.BlockSpec(memory_space=pltpu.HBM)
@@ -51,14 +51,33 @@
     return copies
 
 
+def window_of(chip, chips, blocks):
+    own = blocks // chips
+    size = min(own + 2, own + chips - 1)
+    return jnp.clip(chip * own - 1, 0, blocks - size), size
+
+
+def my_chip():
+    return lax.axis_index("var") // 2
+
+
+def chip_count():
+    return lax.axis_size("var") // 2
+
+
+def lanes(start, size):
+    return pl.ds(pl.multiple_of(start * LANES, LANES), size * LANES)
+
+
 def first_kernel(slots, sens_hbm, factor_hbm, control_hbm, kappa_hbm, tile_hbm, row_hbm, sensor_hbm,
                  value_hbm, weight_hbm, cols_hbm, own_ref, other_ref, response_ref, kappa_ref, *refs):
     chunk_refs = refs[:-12]
     (sens_ref, factor_ref, control_ref, tile_ref, row_ref, sensor_ref, value_ref, weight_ref, cols_ref,
      send_ref, count_ref, sems) = refs[-12:]
+    window = lanes(*window_of(my_chip(), chip_count(), own_ref.shape[1] // LANES))
     pairs = (
         (sens_hbm, sens_ref), (factor_hbm, factor_ref), (control_hbm, control_ref),
-        (kappa_hbm, kappa_ref), (tile_hbm, tile_ref), (row_hbm, row_ref), (sensor_hbm, sensor_ref),
+        (kappa_hbm.at[:, :, window], kappa_ref), (tile_hbm, tile_ref), (row_hbm, row_ref), (sensor_hbm, sensor_ref),
         (value_hbm, value_ref), (weight_hbm, weight_ref), (cols_hbm, cols_ref),
     )
     copies = [pltpu.make_async_copy(src, dst, sems.at[i]) for i, (src, dst) in enumerate(pairs)]
@@ -113,7 +132,7 @@
     return top, values - top
 
 
-def scatter_kernel(slots, after_ref, home_ref, *refs):
+def scatter_kernel(slots, blocks_all, after_ref, home_ref, *refs):
     got_refs, (own_ref, other_ref, first_ref, acc_ref, meta_ref, sems) = refs[:-6], refs[-6:]
     core = lax.axis_index("var") % 2
     first_ref[...] = jnp.where(core == 0, home_ref[...], got_refs[0][...])
@@ -124,13 +143,18 @@
     ]
     for copy in copies:
         copy.start()
-    rows, width_cols = own_ref.shape[1:]
-    blocks = width_cols // LANES
+    rows = own_ref.shape[1]
+    start, size = window_of(my_chip(), chip_count(), blocks_all)
+    per_kind = padded_blocks(size)
+    tall = 2 * per_kind
     acc_ref[...] = jnp.zeros(acc_ref.shape, F32)
-    block_ids = lax.broadcasted_iota(jnp.int32, (blocks, LANES), 0)
+    place = lax.broadcasted_iota(jnp.int32, (tall, LANES), 0)
+    is_weight = place < per_kind
+    place = jnp.where(is_weight, place, place - per_kind) + start
     lane_ids = lax.broadcasted_iota(jnp.int32, (LANES, LANES), 0).astype(F32).astype(jnp.bfloat16)
     one, zero = jnp.bfloat16(1), jnp.bfloat16(0)
     sub = lax.broadcasted_iota(jnp.int32, (GROUP, LANES), 0)
+    blank = jnp.zeros((2 * tall, LANES), jnp.bfloat16)
     for copy in copies:
         copy.wait()
 
@@ -143,23 +167,38 @@
             weight = got_ref[pl.ds(slots + base, GROUP), :]
             cell = got_ref[pl.ds(2 * slots + base, GROUP), :].astype(jnp.int32)
             weight = jnp.where(sub + base < count, weight, 0.0)
-            parts = pieces(weight) + pieces(weight * value)
+            parts = (pieces(weight), pieces(weight * value))
             low = (cell % LANES).astype(F32)
             high = cell // LANES
-            for k in range(GROUP):
-                in_block = block_ids == high[k : k + 1]
+            for k in range(0, GROUP, 2):
+                left, right = [], []
+                for i in (k, k + 1):
+                    here = place == high[i : i + 1]
+                    rows_of = [
+                        jnp.where(here, jnp.where(is_weight, w[i : i + 1], v[i : i + 1]), 0.0)
+                        for w, v in zip(*parts)
+                    ]
+                    left.append(jnp.concatenate(rows_of, axis=0).astype(jnp.bfloat16))
+                    column = jnp.broadcast_to(low[i : i + 1], (16, LANES)).astype(jnp.bfloat16)
+                    column = jnp.concatenate([column] * (LANES // 16), axis=0)
+                    right.append(jnp.where(lane_ids == column, one, zero))
                 left = jnp.concatenate(
-                    [jnp.where(in_block, parts[i][k : k + 1], 0.0) for i in (0, 2, 1, 3)], axis=0
-                ).astype(jnp.bfloat16)
-                column = jnp.broadcast_to(low[k : k + 1], (16, LANES)).astype(jnp.bfloat16)
-                right = jnp.where(lane_ids == jnp.concatenate([column] * (LANES // 16), axis=0), one, zero)
+                    [
+                        jnp.concatenate([left[0], blank], axis=1),
+                        jnp.concatenate([blank, left[1]], axis=1),
+                    ],
+                    axis=0,
+                )
                 both = lax.dot_general(
-                    left, right, (((1,), (1,)), ((), ())), preferred_element_type=F32
+                    left, jnp.concatenate(right, axis=1), (((1,), (1,)), ((), ())),
+                    preferred_element_type=F32,
                 )
-                row = meta_ref[8 * s, base + k].astype(jnp.int32)
-                sensor = meta_ref[8 * s + 1, base + k].astype(jnp.int32)
-                at = pl.multiple_of((sensor * rows + row) * 2 * blocks, 2 * blocks)
-                acc_ref[pl.ds(at, 2 * blocks), :] += both[: 2 * blocks] + both[2 * blocks :]
+                for i in (0, 1):
+                    row = meta_ref[8 * s, base + k + i].astype(jnp.int32)
+                    sensor = meta_ref[8 * s + 1, base + k + i].astype(jnp.int32)
+                    at = pl.multiple_of((sensor * rows + row) * tall, 8)
+                    mine = both[2 * i * tall : 2 * (i + 1) * tall]
+                    acc_ref[pl.ds(at, tall), :] += mine[:tall] + mine[tall:]
             return carry
 
         lax.fori_loop(0, (count + GROUP - 1) // GROUP, group, 0)
@@ -167,12 +206,16 @@
     for s, got_ref in enumerate(got_refs):
         source(s, got_ref)
     for sensor, out_ref in ((core, own_ref), (1 - core, other_ref)):
-        start = sensor * rows * 2 * blocks
+        begin = sensor * rows * tall
         for kind in range(2):
-            for b in range(blocks):
+            for b in range(size):
                 out_ref[kind, :, b * LANES : (b + 1) * LANES] = acc_ref[
-                    pl.ds(start + kind * blocks + b, rows, stride=2 * blocks), :
+                    pl.ds(begin + kind * per_kind + b, rows, stride=tall), :
                 ]
+
+
+def padded_blocks(size):
+    return -(-size // 4) * 4
 
 
 def even_tile():
@@ -197,9 +240,18 @@
         odd_ref[b * margin : (b + 1) * margin] = jnp.where(even, head, tail)
 
 
-def edges_kernel(margin, first_ref, second_ref, kappa_ref, *refs):
-    total_ref, even_ref, odd_ref = refs[-3:]
-    total = first_ref[...] + second_ref[...]
+def cut_kernel(first_ref, second_ref, mine_ref, *out_refs):
+    chip, chips, blocks = my_chip(), chip_count(), first_ref.shape[1] // LANES
+    for d, out_ref in enumerate((mine_ref, *out_refs)):
+        window = lanes(*window_of(chip ^ d, chips, blocks))
+        out_ref[...] = first_ref[:, window] + second_ref[:, window]
+
+
+def edges_kernel(margin, chips, kappa_ref, *refs):
+    terms, (total_ref, even_ref, odd_ref) = refs[:chips], refs[-3:]
+    total = terms[0][...]
+    for term in terms[1:]:
+        total = total + term[...]
     total_ref[...] = total
     for i, field in enumerate((total, kappa_ref[0], kappa_ref[1])):
         pack_edges(even_ref.at[i], odd_ref.at[i], field, margin)
@@ -325,7 +377,8 @@
 def adjoint_kernel(margin, smooth_ref, mask_ref, sums_ref, more_ref, adjoint_ref, even_ref, odd_ref):
     weight = sums_ref[0] + more_ref[0]
     value = sums_ref[1] + more_ref[1]
-    adjoint = mask_ref[...].astype(F32) * (weight * smooth_ref[...] - value)
+    window = lanes(*window_of(my_chip(), chip_count(), mask_ref.shape[1] // LANES))
+    adjoint = mask_ref[:, window].astype(F32) * (weight * smooth_ref[...] - value)
     adjoint_ref[...] = adjoint
     pack_edges(even_ref, odd_ref, adjoint, margin)
 
@@ -334,7 +387,16 @@
     rows = own_ref.shape[0]
     lay_ring(one_ref, own_ref[...], even_ref, odd_ref, margin)
     diffuse(one_ref, two_ref, coef_ref, rows, margin)
-    out_ref[...] = one_ref[:rows]
+    own = out_ref.shape[1] // LANES
+    start = window_of(my_chip(), chip_count(), own * chip_count())[0]
+    out_ref[...] = one_ref[:rows, lanes(my_chip() * own - start, own)]
+
+
+def join_kernel(*refs):
+    out_ref = refs[-1]
+    for d, ref in enumerate(refs[:-1]):
+        own = ref.shape[1] // LANES
+        out_ref[:, lanes((my_chip() ^ d) * own, own)] = ref[...]
 
 
 def result_kernel(response_ref, control_ref, own_ref, other_ref, out_ref):
@@ -357,14 +419,6 @@
             to = other * members + q if 0 <= other < tiles else t * members + (q ^ 1)
             pairs.append((t * members + q, to))
     return swap(even, "tile", 1), lax.ppermute(odd, ("tile", "var"), pairs)
-
-
-def combine(values, members, first):
-    bit = first
-    while 2 * bit < members:
-        values = values + swap(values, "var", bit)
-        bit *= 2
-    return values, swap(values, "var", bit)
 
 
 def deliver(chunk, turn):
@@ -388,16 +442,20 @@
     blocks = width // LANES
     margin = PASSES
     total = ring_rows(rows, margin)
+    chips = members // 2
+    size = window_of(0, chips, blocks)[1]
     field = jax.ShapeDtypeStruct((rows, width), F32)
-    field2 = jax.ShapeDtypeStruct((2, rows, width), F32)
-    edge = jax.ShapeDtypeStruct((margin * blocks, LANES), F32)
-    edge3 = jax.ShapeDtypeStruct((3, margin * blocks, LANES), F32)
+    share = jax.ShapeDtypeStruct((rows, width // chips), F32)
+    view = jax.ShapeDtypeStruct((rows, size * LANES), F32)
+    view2 = jax.ShapeDtypeStruct((2, *view.shape), F32)
+    edge = jax.ShapeDtypeStruct((margin * size, LANES), F32)
+    edge3 = jax.ShapeDtypeStruct((3, *edge.shape), F32)
     chunk = jax.ShapeDtypeStruct((3 * slots + 8, panel_width), F32)
     ints = pltpu.SMEM((panels,), jnp.int32)
 
     own, other, responses, kappa, *chunks = call(
         functools.partial(first_kernel, slots),
-        [field, field, jax.ShapeDtypeStruct((2, var_dev, 8, LANES), F32), field2] + [chunk] * turns,
+        [field, field, jax.ShapeDtypeStruct((2, var_dev, 8, LANES), F32), view2] + [chunk] * turns,
         [HBM] * 10,
         [
             pltpu.SMEM(sensitivity.shape, F32),
@@ -416,30 +474,33 @@
                             panel_row, panel_sensor, obs_values, obs_weights, panel_cols)))
 
     got = [deliver(c, turn) for turn, c in enumerate(chunks)]
-    part, more = combine(own + swap(other, "var", 1), members, 2)
+    part, *parts = call(cut_kernel, [view] * chips, [VMEM] * 2, cost=cost(200))(
+        own, swap(other, "var", 1)
+    )
+    parts = [swap(p, "var", 2 * (d + 1)) for d, p in enumerate(parts)]
     smooth_in, even, odd = call(
-        functools.partial(edges_kernel, margin),
-        [field, edge3, edge3],
-        [VMEM] * 3 + [AFTER] * turns,
+        functools.partial(edges_kernel, margin, chips),
+        [view, edge3, edge3],
+        [VMEM] * (1 + chips) + [AFTER] * turns,
         cost=cost(500),
-    )(part, more, kappa, *got)
+    )(kappa, part, *parts, *got)
     even, odd = swap_edges(even, odd)
     sums, sums_other = call(
-        functools.partial(scatter_kernel, slots),
-        [field2, field2],
+        functools.partial(scatter_kernel, slots, blocks),
+        [view2, view2],
         [AFTER] + [VMEM] * (turns + 1),
         [
             pltpu.VMEM(chunk.shape, F32),
-            pltpu.VMEM((2 * rows * 2 * blocks, LANES), F32),
+            pltpu.VMEM((2 * rows * 2 * padded_blocks(size), LANES), F32),
             pltpu.SMEM((8 * turns, LANES), F32),
             pltpu.SemaphoreType.DMA((turns,)),
         ],
         cost=cost(10000),
     )(smooth_in, chunks[0], *got)
-    ring = pltpu.VMEM((total, width), F32)
+    ring = pltpu.VMEM((total, size * LANES), F32)
     coef, sums_other = call(
         functools.partial(faces_kernel, margin),
-        [jax.ShapeDtypeStruct((5, total, width), F32), field2],
+        [jax.ShapeDtypeStruct((5, total, size * LANES), F32), view2],
         [VMEM] * 4,
         [ring, ring],
         cost=cost(1000),
@@ -447,22 +508,24 @@
     more_sums = swap(sums_other, "var", 1)
     (smooth,) = call(
         functools.partial(smooth_kernel, margin),
-        [field],
+        [view],
         [VMEM] * 4,
         [ring, ring],
         cost=cost(4000),
     )(smooth_in, even, odd, coef)
     adjoint, even, odd = call(
-        functools.partial(adjoint_kernel, margin), [field, edge, edge], [VMEM] * 4, cost=cost(500)
+        functools.partial(adjoint_kernel, margin), [view, edge, edge], [VMEM] * 4, cost=cost(500)
     )(smooth, land_mask, sums, more_sums)
     even, odd = swap_edges(even, odd)
     (mine,) = call(
         functools.partial(spread_kernel, margin),
-        [field],
+        [share],
         [VMEM] * 4,
         [ring, ring],
         cost=cost(4000),
     )(adjoint, even, odd, coef)
+    shares = [mine] + [swap(mine, "var", 2 * d) for d in range(1, chips)]
+    (mine,) = call(join_kernel, [field], [VMEM] * chips, cost=cost(200))(*shares)
     (out,) = call(
         result_kernel,
         [jax.ShapeDtypeStruct(control.shape, F32)],

time: 35.4 us -> 33 us (0.932)
  waiting for transfers between devices: 14.4 us -> 12.1 us
  Pallas kernels: 10.4 us -> 8.57 us
  starting transfers between devices: 10.3 us -> 12.1 us
    pallas_call x5 -> x7, Pallas kernels: 6.84 us -> 5.14 us  [the longest x1 2.12 us: local(): call(functools.partial(scatter_kernel, slots, blocks), [view2, view2], [A...]
    ppermute x2, waiting for transfers between devices: 4.99 us -> 3.57 us  [deliver(): return lax.ppermute(chunk, ('tile', 'var'), pairs)]
    ppermute x6 -> x7, waiting for transfers between devices: 9.42 us -> 8.5 us  [swap(): return lax.ppermute(values, axis, [(i, i ^ bit) for i in range(count)])]
    ppermute x6 -> x7, starting transfers between devices: 8.03 us -> 8.78 us  [swap(): return lax.ppermute(values, axis, [(i, i ^ bit) for i in range(count)])]
    ppermute x2, starting transfers between devices: 2.03 us -> 2.73 us  [deliver(): return lax.ppermute(chunk, ('tile', 'var'), pairs)]
  transfers between devices with their start and end apart: 10 -> 11, of which waited for: 6 -> 6; matrix products, arithmetic and copies ran while one was open for 0% -> 0% of each run, Pallas kernels for 14% -> 11%
where the time goes in v1:
time: 33 us; the launch traced here: 32.8 us
  starting transfers between devices  12.1 us (37%)
  waiting for transfers between devices  12.1 us (37%)
  Pallas kernels  8.57 us (26%)
    ppermute x7, starting transfers between devices, swap(): return lax.ppermute(values, axis, [(i, i ^ bit) for i in range(count)])  8.78 us
    ppermute x7, waiting for transfers between devices, swap(): return lax.ppermute(values, axis, [(i, i ^ bit) for i in range(count)])  8.5 us
    ppermute x2, waiting for transfers between devices, deliver(): return lax.ppermute(chunk, ('tile', 'var'), pairs)  3.57 us
    ppermute x2, starting transfers between devices, deliver(): return lax.ppermute(chunk, ('tile', 'var'), pairs)  2.73 us
    pallas_call x1, Pallas kernels, local(): call(functools.partial(first_kernel, slots), [field, field, jax.ShapeDtyp...  2.44 us
    pallas_call x1, Pallas kernels, local(): call(functools.partial(scatter_kernel, slots, blocks), [view2, view2], [A...  2.12 us
    pallas_call x1, Pallas kernels, local(): call(functools.partial(spread_kernel, margin), [share], [VMEM] * 4, [ring...  1.45 us
    pallas_call x1, Pallas kernels, local(): call(functools.partial(smooth_kernel, margin), [view], [VMEM] * 4, [ring,...  1.44 us
  transfers between devices with their start and end apart: 11, of which 6 were waited for; matrix products, arithmetic and copies ran while one was open for 0% of the time, Pallas kernels for 11%

profile of v1, /device:TPU:0, one launch (start us, length us, event | category | flops | bytes accessed | tf_op | source)
XLA Modules:
  0.0 32.8 jit_solution(12212050218462230240)
XLA Ops:
  0.0 2.4 %shard_map.109 = (f32[16,2048]{1,0:T(8,128)S(1)}, f32[16,2048]{1,0:T(8,128)S(1)}, f32[2,2,8,128]{3,2,1,0:T(8,128)S(1)}, f32[2,16,1152]{2,1,0:T(8,128)S(1)}, f32[...) custom-call(f32[2,8]{1,0:T(2,128)} %sens_hbm.1, f32[8,8]{1,0:T(8,128)} %factor_hbm.1, f32[2,16,2048]{2,1,0:T(8,128)} %control_ref.1, ...), custom_call_target="tpu_custom_call" | custom-call | flops 12288000 | bytes 3072000 | tf_op jit(solution)/shard_map/pallas_call | solution.py:456
  2.4 0.5 %collective-permute-start = (f32[16,2048]{1,0:T(8,128)S(1)}, f32[16,2048]{1,0:T(8,128)S(1)}, u32[]{:S(2)}, u32[]{:S(2)}) collective-permute-start(f32[16,2048]{1,0:T(8,128)S(1)} %get-tuple-element.26), channel_id=1, source_target_pairs={{0,1},{1,0},{2,3},{3,2},{4,5},{5,4},{6,7},{7,6},{8,9},{9,8},{10,11... | collective-permute-start | bytes 393224 | tf_op jit(solution)/shard_map/ppermute | solution.py:410
  3.0 2.6 %collective-permute-start.3 = (f32[200,128]{1,0:T(8,128)S(1)}, f32[200,128]{1,0:T(8,128)S(1)}, u32[]{:S(2)}, u32[]{:S(2)}) collective-permute-start(f32[200,128]{1,0:T(8,128)S(1)} %get-tuple-element.30), channel_id=1, source_target_pairs={{0,4},{1,13},{2,6},{3,15},{4,0},{5,9},{6,2},{7,11},{8,12},{9,5},{1... | collective-permute-start | bytes 307208 | tf_op jit(solution)/shard_map/ppermute | solution.py:431
  5.6 0.1 collective-permute-start.2
  5.7 0.0 collective-permute-done.second_ref
  5.7 1.9 %collective-permute-start.1 = (f32[16,1152]{1,0:T(8,128)S(1)}, f32[16,1152]{1,0:T(8,128)S(1)}, u32[]{:S(2)}, u32[]{:S(2)}) collective-permute-start(f32[16,1152]{1,0:T(8,128)S(1)} %get-tuple-element.28), channel_id=1, source_target_pairs={{0,2},{1,3},{2,0},{3,1},{4,6},{5,7},{6,4},{7,5},{8,10},{9,11},{10,... | collective-permute-start | bytes 221192 | tf_op jit(solution)/shard_map/ppermute | solution.py:410
  7.6 0.6 %collective-permute-done.3.refs_3_.refs_1_ = f32[200,128]{1,0:T(8,128)S(1)} collective-permute-done((f32[200,128]{1,0:T(8,128)S(1)}, f32[200,128]{1,0:T(8,128)S(1)}, u32[]{:S(2)}, u32[]{:S(2)}) %collective-permute-start.3) | collective-permute-done | bytes 102432 | tf_op jit(solution)/shard_map/ppermute | solution.py:431
  8.3 3.0 %collective-permute-done.2.refs_2_.refs_0_ = f32[200,128]{1,0:T(8,128)S(1)} collective-permute-done((f32[200,128]{1,0:T(8,128)S(1)}, f32[200,128]{1,0:T(8,128)S(1)}, u32[]{:S(2)}, u32[]{:S(2)}) %collective-permute-start.2) | collective-permute-done | bytes 102432 | tf_op jit(solution)/shard_map/ppermute | solution.py:431
  11.2 0.0 collective-permute-done.1.refs_1_
  11.3 1.5 %collective-permute-start.4 = (f32[3,90,128]{2,1,0:T(8,128)S(1)}, f32[3,90,128]{2,1,0:T(8,128)S(1)}, u32[]{:S(2)}, u32[]{:S(2)}) collective-permute-start(f32[3,90,128]{2,1,0:T(8,128)S(1)} %get-tuple-element.32), channel_id=1, source_target_pairs={{0,4},{4,0},{8,12},{12,8},{1,5},{5,1},{9,13},{13,9},{2,6},{6,2},{1... | collective-permute-start | bytes 414728 | tf_op jit(solution)/shard_map/ppermute | solution.py:410
  12.7 0.3 %collective-permute-start.5 = (f32[3,90,128]{2,1,0:T(8,128)S(1)}, f32[3,90,128]{2,1,0:T(8,128)S(1)}, u32[]{:S(2)}, u32[]{:S(2)}) collective-permute-start(f32[3,90,128]{2,1,0:T(8,128)S(1)} %get-tuple-element.33), channel_id=1, source_target_pairs={{0,1},{1,0},{2,3},{3,2},{4,8},{5,9},{6,10},{7,11},{8,4},{9,5},{10,... | collective-permute-start | bytes 414728 | tf_op jit(solution)/shard_map/ppermute | solution.py:421
  13.1 2.1 %shard_map.112 = (f32[2,16,1152]{2,1,0:T(8,128)S(1)}, f32[2,16,1152]{2,1,0:T(8,128)S(1)}) custom-call(f32[16,1152]{1,0:T(8,128)S(1)} %get-tuple-element.31.after_ref.own_ref, f32[200,128]{1,0:T(8,128)S(1)} %get-tuple-element.29.home_ref, f32[200,128]{1,0:T(8,128)S(1)} %collective-permute-done.2.refs_2_.refs_0_, ...), custom_call_target="tpu_custom_call" | custom-call | flops 40960000 | bytes 10240000 | tf_op jit(solution)/shard_map/pallas_call | solution.py:488
  15.2 2.2 %collective-permute-done.4.even_ref = f32[3,90,128]{2,1,0:T(8,128)S(1)} collective-permute-done((f32[3,90,128]{2,1,0:T(8,128)S(1)}, f32[3,90,128]{2,1,0:T(8,128)S(1)}, u32[]{:S(2)}, u32[]{:S(2)}) %collective-permute-start.4) | collective-permute-done | bytes 138272 | tf_op jit(solution)/shard_map/ppermute | solution.py:410
  17.4 0.0 collective-permute-done.5.odd_ref
  17.4 0.2 shard_map.113
  17.6 0.5 %collective-permute-start.6 = (f32[2,16,1152]{2,1,0:T(8,128)S(1)}, f32[2,16,1152]{2,1,0:T(8,128)S(1)}, u32[]{:S(2)}, u32[]{:S(2)}) collective-permute-start(f32[2,16,1152]{2,1,0:T(8,128)S(1)} %get-tuple-element.37), channel_id=1, source_target_pairs={{0,1},{1,0},{2,3},{3,2},{4,5},{5,4},{6,7},{7,6},{8,9},{9,8},{10,11... | collective-permute-start | bytes 442376 | tf_op jit(solution)/shard_map/ppermute | solution.py:410
  18.2 0.0 copy-start.1
  18.2 1.4 %shard_map.114.smooth_ref = f32[16,1152]{1,0:T(8,128)S(1)} custom-call(f32[16,1152]{1,0:T(8,128)S(1)} %get-tuple-element.31.after_ref.own_ref, f32[3,90,128]{2,1,0:T(8,128)S(1)} %collective-permute-done.4.even_ref, f32[3,90,128]{2,1,0:T(8,128)S(1)} %collective-permute-done.5.odd_ref, f32[5,40,1152]{2,1,0:T(8,128)S(1)} %get-tuple-element.35.coef_ref), custom_call_target="tpu_custom_call" | custom-call | flops 16384000 | bytes 4096000 | tf_op jit(solution)/shard_map/pallas_call | solution.py:509
  19.6 0.0 collective-permute-done.6.more_ref
  19.6 0.0 copy-done.1
  19.7 2.7 %collective-permute-start.7 = (f32[90,128]{1,0:T(8,128)S(1)}, f32[90,128]{1,0:T(8,128)S(1)}, u32[]{:S(2)}, u32[]{:S(2)}) collective-permute-start(f32[90,128]{1,0:T(8,128)S(1)} %get-tuple-element.39), channel_id=1, source_target_pairs={{0,4},{4,0},{8,12},{12,8},{1,5},{5,1},{9,13},{13,9},{2,6},{6,2},{1... | collective-permute-start | bytes 138248 | tf_op jit(solution)/shard_map/ppermute | solution.py:410
  22.4 0.2 collective-permute-start.8
  22.6 2.2 %collective-permute-done.7.even_ref = f32[90,128]{1,0:T(8,128)S(1)} collective-permute-done((f32[90,128]{1,0:T(8,128)S(1)}, f32[90,128]{1,0:T(8,128)S(1)}, u32[]{:S(2)}, u32[]{:S(2)}) %collective-permute-start.7) | collective-permute-done | bytes 46112 | tf_op jit(solution)/shard_map/ppermute | solution.py:410
  24.8 0.0 collective-permute-done.8.odd_ref
  24.8 1.5 %shard_map.116.refs_0_ = f32[16,1024]{1,0:T(8,128)S(1)} custom-call(f32[16,1152]{1,0:T(8,128)S(1)} %get-tuple-element.38.own_ref, f32[90,128]{1,0:T(8,128)S(1)} %collective-permute-done.7.even_ref, f32[90,128]{1,0:T(8,128)S(1)} %collective-permute-done.8.odd_ref, f32[5,40,1152]{2,1,0:T(8,128)S(1)} %get-tuple-element.35.coef_ref), custom_call_target="tpu_custom_call" | custom-call | flops 16384000 | bytes 4096000 | tf_op jit(solution)/shard_map/pallas_call | solution.py:520
  26.2 0.0 copy-start
  26.3 1.6 %collective-permute-start.9 = (f32[16,1024]{1,0:T(8,128)S(1)}, f32[16,1024]{1,0:T(8,128)S(1)}, u32[]{:S(2)}, u32[]{:S(2)}) collective-permute-start(f32[16,1024]{1,0:T(8,128)S(1)} %shard_map.116.refs_0_), channel_id=1, source_target_pairs={{0,2},{1,3},{2,0},{3,1},{4,6},{5,7},{6,4},{7,5},{8,10},{9,11},{10,... | collective-permute-start | bytes 196616 | tf_op jit(solution)/shard_map/ppermute | solution.py:410
  27.8 2.8 %collective-permute-done.9.refs_1_ = f32[16,1024]{1,0:T(8,128)S(1)} collective-permute-done((f32[16,1024]{1,0:T(8,128)S(1)}, f32[16,1024]{1,0:T(8,128)S(1)}, u32[]{:S(2)}, u32[]{:S(2)}) %collective-permute-start.9) | collective-permute-done | bytes 65568 | tf_op jit(solution)/shard_map/ppermute | solution.py:410
  30.6 0.1 collective-permute-start.10
  30.7 1.3 %collective-permute-done.10.other_ref = f32[16,2048]{1,0:T(8,128)S(1)} collective-permute-done((f32[16,2048]{1,0:T(8,128)S(1)}, f32[16,2048]{1,0:T(8,128)S(1)}, u32[]{:S(2)}, u32[]{:S(2)}) %collective-permute-start.10) | collective-permute-done | bytes 131104 | tf_op jit(solution)/shard_map/ppermute | solution.py:410
  32.0 0.0 copy-done
  32.0 0.8 %shard_map.118 = f32[2,16,2048]{2,1,0:T(8,128)} custom-call(f32[2,2,8,128]{3,2,1,0:T(8,128)S(1)} %get-tuple-element.23.response_ref, f32[2,16,2048]{2,1,0:T(8,128)S(1)} %copy-done, f32[16,2048]{1,0:T(8,128)S(1)} %shard_map.117.own_ref, f32[16,2048]{1,0:T(8,128)S(1)} %collective-permute-done.10.other_ref), custom_call_target="tpu_custom_call" | custom-call | flops 4096000 | bytes 1024000 | tf_op jit(solution)/shard_map/pallas_call | solution.py:529
  (4 shorter events, 0.1 us)
Async XLA Ops:
  2.4 3.2 %collective-permute-start = (f32[16,2048]{1,0:T(8,128)S(1)}, f32[16,2048]{1,0:T(8,128)S(1)}, u32[]{:S(2)}, u32[]{:S(2)}) collective-permute-start(f32[16,2048]{1,0:T(8,128)S(1)} %get-tuple-element.26), channel_id=1, source_target_pairs={{0,1},{1,0},{2,3},{3,2},{4,5},{5,4},{6,7},{7,6},{8,9},{9,8},{10,11... | collective-permute-start | bytes 393224 | tf_op jit(solution)/shard_map/ppermute | solution.py:410
  3.0 5.3 %collective-permute-start.3 = (f32[200,128]{1,0:T(8,128)S(1)}, f32[200,128]{1,0:T(8,128)S(1)}, u32[]{:S(2)}, u32[]{:S(2)}) collective-permute-start(f32[200,128]{1,0:T(8,128)S(1)} %get-tuple-element.30), channel_id=1, source_target_pairs={{0,4},{1,13},{2,6},{3,15},{4,0},{5,9},{6,2},{7,11},{8,12},{9,5},{1... | collective-permute-start | bytes 307208 | tf_op jit(solution)/shard_map/ppermute | solution.py:431
  5.6 5.6 %collective-permute-start.2 = (f32[200,128]{1,0:T(8,128)S(1)}, f32[200,128]{1,0:T(8,128)S(1)}, u32[]{:S(2)}, u32[]{:S(2)}) collective-permute-start(f32[200,128]{1,0:T(8,128)S(1)} %get-tuple-element.29.home_ref), channel_id=1, source_target_pairs={{0,4},{1,9},{2,6},{3,11},{4,0},{5,13},{6,2},{7,15},{8,12},{9,1},{1... | collective-permute-start | bytes 307208 | tf_op jit(solution)/shard_map/ppermute | solution.py:431
  5.7 5.5 %collective-permute-start.1 = (f32[16,1152]{1,0:T(8,128)S(1)}, f32[16,1152]{1,0:T(8,128)S(1)}, u32[]{:S(2)}, u32[]{:S(2)}) collective-permute-start(f32[16,1152]{1,0:T(8,128)S(1)} %get-tuple-element.28), channel_id=1, source_target_pairs={{0,2},{1,3},{2,0},{3,1},{4,6},{5,7},{6,4},{7,5},{8,10},{9,11},{10,... | collective-permute-start | bytes 221192 | tf_op jit(solution)/shard_map/ppermute | solution.py:410
  11.3 6.1 %collective-permute-start.4 = (f32[3,90,128]{2,1,0:T(8,128)S(1)}, f32[3,90,128]{2,1,0:T(8,128)S(1)}, u32[]{:S(2)}, u32[]{:S(2)}) collective-permute-start(f32[3,90,128]{2,1,0:T(8,128)S(1)} %get-tuple-element.32), channel_id=1, source_target_pairs={{0,4},{4,0},{8,12},{12,8},{1,5},{5,1},{9,13},{13,9},{2,6},{6,2},{1... | collective-permute-start | bytes 414728 | tf_op jit(solution)/shard_map/ppermute | solution.py:410
  12.7 4.7 %collective-permute-start.5 = (f32[3,90,128]{2,1,0:T(8,128)S(1)}, f32[3,90,128]{2,1,0:T(8,128)S(1)}, u32[]{:S(2)}, u32[]{:S(2)}) collective-permute-start(f32[3,90,128]{2,1,0:T(8,128)S(1)} %get-tuple-element.33), channel_id=1, source_target_pairs={{0,1},{1,0},{2,3},{3,2},{4,8},{5,9},{6,10},{7,11},{8,4},{9,5},{10,... | collective-permute-start | bytes 414728 | tf_op jit(solution)/shard_map/ppermute | solution.py:421
  17.6 2.0 %collective-permute-start.6 = (f32[2,16,1152]{2,1,0:T(8,128)S(1)}, f32[2,16,1152]{2,1,0:T(8,128)S(1)}, u32[]{:S(2)}, u32[]{:S(2)}) collective-permute-start(f32[2,16,1152]{2,1,0:T(8,128)S(1)} %get-tuple-element.37), channel_id=1, source_target_pairs={{0,1},{1,0},{2,3},{3,2},{4,5},{5,4},{6,7},{7,6},{8,9},{9,8},{10,11... | collective-permute-start | bytes 442376 | tf_op jit(solution)/shard_map/ppermute | solution.py:410
  18.2 1.5 %copy-start.1 = (s32[16,2048]{1,0:T(8,128)S(1)}, s32[16,2048]{1,0:T(8,128)}, u32[]{:S(2)}) copy-start(s32[16,2048]{1,0:T(8,128)} %mask_ref.1) | copy-start | bytes 393220
  19.7 5.1 %collective-permute-start.7 = (f32[90,128]{1,0:T(8,128)S(1)}, f32[90,128]{1,0:T(8,128)S(1)}, u32[]{:S(2)}, u32[]{:S(2)}) collective-permute-start(f32[90,128]{1,0:T(8,128)S(1)} %get-tuple-element.39), channel_id=1, source_target_pairs={{0,4},{4,0},{8,12},{12,8},{1,5},{5,1},{9,13},{13,9},{2,6},{6,2},{1... | collective-permute-start | bytes 138248 | tf_op jit(solution)/shard_map/ppermute | solution.py:410
  22.4 2.4 %collective-permute-start.8 = (f32[90,128]{1,0:T(8,128)S(1)}, f32[90,128]{1,0:T(8,128)S(1)}, u32[]{:S(2)}, u32[]{:S(2)}) collective-permute-start(f32[90,128]{1,0:T(8,128)S(1)} %get-tuple-element.40), channel_id=1, source_target_pairs={{0,1},{1,0},{2,3},{3,2},{4,8},{5,9},{6,10},{7,11},{8,4},{9,5},{10,... | collective-permute-start | bytes 138248 | tf_op jit(solution)/shard_map/ppermute | solution.py:421
  26.2 5.8 %copy-start = (f32[2,16,2048]{2,1,0:T(8,128)S(1)}, f32[2,16,2048]{2,1,0:T(8,128)}, u32[]{:S(2)}) copy-start(f32[2,16,2048]{2,1,0:T(8,128)} %control_ref.1) | copy-start | bytes 786436
  26.3 4.3 %collective-permute-start.9 = (f32[16,1024]{1,0:T(8,128)S(1)}, f32[16,1024]{1,0:T(8,128)S(1)}, u32[]{:S(2)}, u32[]{:S(2)}) collective-permute-start(f32[16,1024]{1,0:T(8,128)S(1)} %shard_map.116.refs_0_), channel_id=1, source_target_pairs={{0,2},{1,3},{2,0},{3,1},{4,6},{5,7},{6,4},{7,5},{8,10},{9,11},{10,... | collective-permute-start | bytes 196616 | tf_op jit(solution)/shard_map/ppermute | solution.py:410
  30.6 1.4 %collective-permute-start.10 = (f32[16,2048]{1,0:T(8,128)S(1)}, f32[16,2048]{1,0:T(8,128)S(1)}, u32[]{:S(2)}, u32[]{:S(2)}) collective-permute-start(f32[16,2048]{1,0:T(8,128)S(1)} %shard_map.117.own_ref), channel_id=1, source_target_pairs={{0,1},{1,0},{2,3},{3,2},{4,5},{5,4},{6,7},{7,6},{8,9},{9,8},{10,11... | collective-permute-start | bytes 393224 | tf_op jit(solution)/shard_map/ppermute | solution.py:410
